TPU v7x, 32 devices: a whole 2x2x4 slice. The times are simulated.
32 devices in a mesh: group: 2 (over x), inner: 16 (over z, y, core).
Axes of the slice: x: 2, y: 2, z: 4, core: 2. Of those that a mesh axis runs over, the one named last changes fastest.
Arguments:
- qkv_rows: bfloat16 [4096, 2304], P(('group', 'inner')), parts along dimension 0, may hold values from -8 to 8
- pair_counts: int32 [32, 16], P('group'), parts along dimension 0, may hold values from 0 to 16, as said below
- image_dims: int32 [2, 32], P(None, 'group'), parts along dimension 1, may hold values from 0 to 4, as said below
- block_mask: int32 [32, 7], P(('group', 'inner')), parts along dimension 0, may hold values from 0 to 1, as said below
- out_weight: bfloat16 [768, 1536], replicated, may hold values from -0.21875 to 0.21875
Outputs:
- layer_out: bfloat16 [4096, 1536], P(('group', 'inner')), parts along dimension 0
There are 2 independent parts, one for each index of `group`. A program takes and returns all parts, laid end to end along the dimension named above; an argument that names none is the same for every part. Nothing has to cross between parts.
Inputs may be any that keep to these rules, and one draw needn't show every extreme that they name: `pair_counts`: every row and every column sums to 128, and every row and every column holds an entry equal to 16. `image_dims`: widths are 1, 2 or 4; each image covers at most 4 tiles and some image is 4 tiles high and 1 wide; the tiles of all images sum to 16; images of height 0 stand only after all others. `block_mask`: column 4 - 1 (a tile with itself) is always 1.
All inputs are finite; a program needn't handle non-finite values.
Results may differ from a plain program's by a relative error of at most 0.0093.
Values may be sent and summed in bfloat16 or wider, within the bound.
A program may use at most 64 MiB of HBM per device.

v0:
```python
import math
import jax
import jax.numpy as jnp
from jax import lax
from jax.sharding import PartitionSpec as P

H = 6
HD = 128
TR = 8
TC = 16
SPAN = 4
MAXT = 4
WIN = 7


def from_behind(value, axis, steps):
    count = lax.axis_size(axis)
    pairs = [(source, (source + steps) % count) for source in range(count)]
    return lax.ppermute(value, axis, pairs)


def block_places(blocks, image_dims):
    heights = image_dims[0]
    widths = image_dims[1]
    tile_count = heights * widths
    starts = jnp.cumsum(tile_count) - tile_count
    inside = (starts[None, :] <= blocks[:, None]).astype(jnp.int32)
    image_id = jnp.sum(inside, axis=1) - 1
    picked = jnp.arange(starts.shape[0], dtype=jnp.int32)[None, :] == image_id[:, None]
    first_block = jnp.sum(jnp.where(picked, starts[None, :], 0), axis=1)
    across = jnp.maximum(jnp.sum(jnp.where(picked, widths[None, :], 0), axis=1), 1)
    local_tile = blocks - first_block
    return (image_id, local_tile // across, local_tile % across)


def rotate(rows_in, row_pos, col_pos):
    count = rows_in.shape[0]
    quarter = HD // 4
    frequency = 10000.0 ** (-jnp.arange(quarter, dtype=jnp.float32) / quarter)
    angles = jnp.stack(
        [
            row_pos.astype(jnp.float32)[:, None] * frequency[None, :],
            col_pos.astype(jnp.float32)[:, None] * frequency[None, :],
        ],
        axis=1,
    )
    cosine = jnp.cos(angles)[:, None, :, :]
    sine_part = jnp.sin(angles)[:, None, :, :]
    split_rows = rows_in.astype(jnp.float32).reshape(count, H, 2, 2, quarter)
    leading = split_rows[:, :, :, 0, :]
    trailing = split_rows[:, :, :, 1, :]
    turned = jnp.stack(
        [leading * cosine - trailing * sine_part, trailing * cosine + leading * sine_part], axis=3
    )
    return turned.reshape(count, H * HD).astype(jnp.bfloat16)


def shards(qkv_rows, pair_counts, image_dims, block_mask, out_weight):
    devices = lax.axis_size("inner")
    self_index = lax.axis_index("inner")
    tok_rows = qkv_rows.shape[0]
    full_width = qkv_rows.shape[1]
    inner_width = full_width // 3
    slot_count = 2 * tok_rows // devices
    block_rows = TR * TC
    per_device = tok_rows // block_rows
    reach_count = (SPAN * tok_rows - block_rows + tok_rows - 1) // tok_rows
    score_scale = 1.0 / math.sqrt(HD)
    sent_counts = lax.dynamic_index_in_dim(pair_counts, self_index, 0, keepdims=False)
    taken_counts = lax.dynamic_index_in_dim(pair_counts, self_index, 1, keepdims=False)
    sent_end = jnp.cumsum(sent_counts)
    sent_start = sent_end - sent_counts
    taken_end = jnp.cumsum(taken_counts)
    taken_start = taken_end - taken_counts
    slot_ids = jnp.arange(slot_count, dtype=jnp.int32)
    row_ids = jnp.arange(tok_rows, dtype=jnp.int32)
    peer_ids = jnp.arange(devices, dtype=jnp.int32)
    outgoing = jnp.minimum(sent_start[:, None] + slot_ids[None, :], tok_rows - 1).reshape(-1)
    parcels = jnp.take(qkv_rows, outgoing, axis=0).reshape(devices, slot_count, full_width)
    arrived = lax.all_to_all(parcels, "inner", split_axis=0, concat_axis=0, tiled=True)
    source = jnp.sum((taken_end[None, :] <= row_ids[:, None]).astype(jnp.int32), axis=1)
    is_source = source[:, None] == peer_ids[None, :]
    offset_in = row_ids - jnp.sum(jnp.where(is_source, taken_start[None, :], 0), axis=1)
    incoming = source * slot_count + offset_in
    owned_rows = jnp.take(arrived.reshape(devices * slot_count, full_width), incoming, axis=0)
    query_blocks = self_index * per_device + jnp.arange(per_device, dtype=jnp.int32)
    query_image, tile_row, tile_col = block_places(query_blocks, image_dims)
    within = jnp.arange(block_rows, dtype=jnp.int32)
    row_pos = (tile_row[:, None] * TR + within[None, :] // TC).reshape(-1)
    col_pos = (tile_col[:, None] * TC + within[None, :] % TC).reshape(-1)
    queries = rotate(owned_rows[:, :inner_width], row_pos, col_pos).reshape(tok_rows, H, HD)
    keys = rotate(owned_rows[:, inner_width : 2 * inner_width], row_pos, col_pos)
    key_value = jnp.stack([keys, owned_rows[:, 2 * inner_width :]])

    def absorb(softmax_state, key_piece, allowed):
        row_max, row_sum, summed = softmax_state
        visible = jnp.repeat(jnp.repeat(allowed, block_rows, axis=0), block_rows, axis=1)[
            :, None, :
        ]
        far_keys = key_piece[0].reshape(tok_rows, H, HD)
        far_values = key_piece[1].reshape(tok_rows, H, HD)
        scores = (
            jnp.einsum("qhd,khd->qhk", queries, far_keys, preferred_element_type=jnp.float32)
            * score_scale
        )
        scores = jnp.where(visible, scores, -1e30)
        new_max = jnp.maximum(row_max, jnp.max(scores, axis=2))
        weights = jnp.where(visible, jnp.exp(scores - new_max[:, :, None]), 0.0)
        rescale = jnp.exp(row_max - new_max)
        row_sum = row_sum * rescale + jnp.sum(weights, axis=2)
        summed = summed * rescale[:, :, None] + jnp.einsum(
            "qhk,khd->qhd",
            weights.astype(jnp.bfloat16),
            far_values,
            preferred_element_type=jnp.float32,
        )
        return (new_max, row_sum, summed)

    def visit(softmax_state, key_piece, source_dev):
        key_blocks = source_dev * per_device + jnp.arange(per_device, dtype=jnp.int32)
        key_image = block_places(key_blocks, image_dims)[0]
        offset = key_blocks[None, :] - query_blocks[:, None] + (MAXT - 1)
        mask_bits = jnp.take_along_axis(block_mask, jnp.clip(offset, 0, WIN - 1), axis=1)
        allowed = (
            (offset >= 0)
            & (offset < WIN)
            & (mask_bits == 1)
            & (query_image[:, None] == key_image[None, :])
            & (source_dev >= 0)
            & (source_dev < devices)
        )
        return absorb(softmax_state, key_piece, allowed)

    initial = (
        jnp.full((tok_rows, H), -1e30, jnp.float32),
        jnp.zeros((tok_rows, H), jnp.float32),
        jnp.zeros((tok_rows, H, HD), jnp.float32),
    )
    farthest = from_behind(key_value, "inner", -reach_count)
    softmax_state = visit(initial, farthest, self_index + reach_count)

    def one_way(hop_index, carry):
        key_piece, running = carry
        key_piece = from_behind(key_piece, "inner", 1)
        return (key_piece, visit(running, key_piece, self_index + reach_count - hop_index - 1))

    softmax_state = lax.fori_loop(0, 2 * reach_count, one_way, (farthest, softmax_state))[1]
    row_max, row_sum, summed = softmax_state
    attended = (summed / row_sum[:, :, None]).reshape(tok_rows, H * HD).astype(jnp.bfloat16)
    projected = jnp.dot(attended, out_weight, preferred_element_type=jnp.float32).astype(
        jnp.bfloat16
    )
    out_width = projected.shape[1]
    back_slots = jnp.minimum(taken_start[:, None] + slot_ids[None, :], tok_rows - 1).reshape(-1)
    returning = jnp.take(projected, back_slots, axis=0).reshape(devices, slot_count, out_width)
    returned = lax.all_to_all(returning, "inner", split_axis=0, concat_axis=0, tiled=True)
    target = jnp.sum((sent_end[None, :] <= row_ids[:, None]).astype(jnp.int32), axis=1)
    is_target = target[:, None] == peer_ids[None, :]
    offset_back = row_ids - jnp.sum(jnp.where(is_target, sent_start[None, :], 0), axis=1)
    return jnp.take(
        returned.reshape(devices * slot_count, out_width), target * slot_count + offset_back, axis=0
    )


def solution(mesh):
    in_specs = (
        P(("group", "inner"), None),
        P("group", None),
        P(None, "group"),
        P(("group", "inner"), None),
        P(),
    )
    out_specs = P(("group", "inner"), None)
    return jax.shard_map(shards, mesh=mesh, in_specs=in_specs, out_specs=out_specs, check_vma=False)
```

profile of v0, /device:TPU:11, one launch (start us, length us, event | category | flops | bytes accessed | tf_op | source)
XLA Modules:
  0.0 164.5 jit_solution(5951095822573143242)
XLA Ops:
  0.0 0.8 fusion.36
  1.6 0.7 bitcast_subtract_fusion.3
  2.5 3.7 %gather_fusion = bf16[256,2304]{1,0:T(8,128)(2,1)S(1)} fusion(bf16[128,2304]{1,0:T(8,128)(2,1)} %param.7, s32[1024]{0:T(1024)S(1)} %pad_clamp_fusion.3), kind=kCustom, calls=%fused_computation | custom fusion | bytes 2360320 | tf_op jit(solution)/shard_map/jit(_take)/gather | solution.py:79
  6.3 1.2 broadcast_select_fusion
  7.4 6.7 %all-to-all-start = ((bf16[16,16,2304]{2,1,0:T(8,128)(2,1)}), bf16[16,16,2304]{2,1,0:T(8,128)(2,1)S(1)}, u32[]{:S(2)}, u32[]{:S(2)}) async-start(bf16[16,16,2304]{2,1,0:T(8,128)(2,1)} %broadcast_select_fusion), calls=%async_computation | async-start | bytes 2359296 | tf_op jit(solution)/shard_map/all_to_all | solution.py:80
  14.2 0.7 reduce-window_2_clone.1
  14.9 1.4 fusion.28
  16.9 0.7 fusion.29
  18.2 0.6 fusion.27
  19.6 0.7 constant_dynamic-slice_fusion.1
  20.3 0.7 reduce-window.13
  21.0 0.8 subtract_reduce_fusion
  22.3 0.6 min.60
  23.0 0.7 sub.186
  23.7 0.7 convert_reduce_fusion
  24.6 0.8 fusion.21
  25.9 0.7 compare_select_fusion.2
  26.6 15.2 %all-to-all-done = bf16[16,16,2304]{2,1,0:T(8,128)(2,1)S(1)} async-done(((bf16[16,16,2304]{2,1,0:T(8,128)(2,1)}), bf16[16,16,2304]{2,1,0:T(8,128)(2,1)S(1)}, u32[]{:S(2)}, u32[]{:S(2)}) %all-to-all-start) | async-done | bytes 1179680 | tf_op jit(solution)/shard_map/all_to_all | solution.py:80
  41.7 1.8 %gather_fusion.1 = bf16[128,2304]{1,0:T(8,128)(2,1)} fusion(bf16[256,2304]{1,0:T(8,128)(2,1)S(1)} %bitcast.110, s32[1024]{0:T(1024)S(1)} %pad_clamp_fusion.2), kind=kCustom, calls=%fused_computation.1 | custom fusion | bytes 1180160 | tf_op jit(solution)/shard_map/jit(_take)/gather | solution.py:85
  43.5 1.2 broadcast_select_fusion.2
  44.7 0.7 slice_convert_fusion
  45.8 1.6 subtract_convert_fusion
  47.6 0.8 pad_maximum_fusion
  50.9 0.6 compare_and_fusion.1
  51.8 7.9 %collective-permute-done.1 = bf16[2,128,768]{2,1,0:T(8,128)(2,1)S(1)} collective-permute-done((bf16[2,128,768]{2,1,0:T(8,128)(2,1)}, bf16[2,128,768]{2,1,0:T(8,128)(2,1)S(1)}, u32[]{:S(2)}, u32[]{:S(2)}) %collective-permute-start.1) | collective-permute-done | bytes 393248 | tf_op jit(solution)/shard_map/ppermute | solution.py:19
  59.7 0.7 fusion.41
  60.4 0.8 copy.38
  61.2 1.2 fusion.42
  63.1 1.1 copy.42
  64.2 1.6 fusion.11
  65.8 1.2 copy.45
  67.0 0.9 copy.44
  68.0 53.5 %while.24 = (s32[]{:T(128)}, bf16[2,128,768]{1,2,0:T(8,128)(2,1)}, f32[128,6]{0,1:T(8,128)S(1)}, f32[128,6]{0,1:T(8,128)S(1)}, f32[128,6,128]{2,0,1:T(8,128)S(1)...) while((s32[]{:T(128)}, bf16[2,128,768]{1,2,0:T(8,128)(2,1)}, ...), condition=%wide.region_17.18_spmd, body=%wide.region_13.17_spmd.sunk | while | flops 51414596 | bytes 5751247 | solution.py:147
  68.0 2.2 %collective-permute-start = (bf16[2,128,768]{1,2,0:T(8,128)(2,1)}, bf16[2,128,768]{1,2,0:T(8,128)(2,1)S(1)}, u32[]{:S(2)}, u32[]{:S(2)}) collective-permute-start(bf16[2,128,768]{1,2,0:T(8,128)(2,1)} %get-tuple-element.481), channel_id=1, source_target_pairs={{0,1},{1,2},{2,3},{3,4},{4,5},{5,6},{6,7},{7,8},{8,9},{9,10},{10,1... | collective-permute-start | bytes 1179656 | tf_op jit(solution)/shard_map/while/body/eval_jaxpr/ppermute | solution.py:19
  70.2 0.6 fusion.67
  71.4 0.6 fusion.66
  72.7 2.5 %collective-permute-done = bf16[2,128,768]{1,2,0:T(8,128)(2,1)S(1)} collective-permute-done((bf16[2,128,768]{1,2,0:T(8,128)(2,1)}, bf16[2,128,768]{1,2,0:T(8,128)(2,1)S(1)}, u32[]{:S(2)}, u32[]{:S(2)}) %collective-permute-start) | collective-permute-done | bytes 393248 | tf_op jit(solution)/shard_map/while/body/eval_jaxpr/ppermute | solution.py:19
  76.0 0.7 copy.65
  76.7 2.4 %collective-permute-start = (bf16[2,128,768]{1,2,0:T(8,128)(2,1)}, bf16[2,128,768]{1,2,0:T(8,128)(2,1)S(1)}, u32[]{:S(2)}, u32[]{:S(2)}) collective-permute-start(bf16[2,128,768]{1,2,0:T(8,128)(2,1)} %get-tuple-element.481), channel_id=1, source_target_pairs={{0,1},{1,2},{2,3},{3,4},{4,5},{5,6},{6,7},{7,8},{8,9},{9,10},{10,1... | collective-permute-start | bytes 1179656 | tf_op jit(solution)/shard_map/while/body/eval_jaxpr/ppermute | solution.py:19
  79.1 0.6 fusion.67
  81.6 2.5 %collective-permute-done = bf16[2,128,768]{1,2,0:T(8,128)(2,1)S(1)} collective-permute-done((bf16[2,128,768]{1,2,0:T(8,128)(2,1)}, bf16[2,128,768]{1,2,0:T(8,128)(2,1)S(1)}, u32[]{:S(2)}, u32[]{:S(2)}) %collective-permute-start) | collective-permute-done | bytes 393248 | tf_op jit(solution)/shard_map/while/body/eval_jaxpr/ppermute | solution.py:19
  84.9 0.7 copy.65
  85.7 2.4 %collective-permute-start = (bf16[2,128,768]{1,2,0:T(8,128)(2,1)}, bf16[2,128,768]{1,2,0:T(8,128)(2,1)S(1)}, u32[]{:S(2)}, u32[]{:S(2)}) collective-permute-start(bf16[2,128,768]{1,2,0:T(8,128)(2,1)} %get-tuple-element.481), channel_id=1, source_target_pairs={{0,1},{1,2},{2,3},{3,4},{4,5},{5,6},{6,7},{7,8},{8,9},{9,10},{10,1... | collective-permute-start | bytes 1179656 | tf_op jit(solution)/shard_map/while/body/eval_jaxpr/ppermute | solution.py:19
  88.1 0.6 fusion.67
  90.6 2.5 %collective-permute-done = bf16[2,128,768]{1,2,0:T(8,128)(2,1)S(1)} collective-permute-done((bf16[2,128,768]{1,2,0:T(8,128)(2,1)}, bf16[2,128,768]{1,2,0:T(8,128)(2,1)S(1)}, u32[]{:S(2)}, u32[]{:S(2)}) %collective-permute-start) | collective-permute-done | bytes 393248 | tf_op jit(solution)/shard_map/while/body/eval_jaxpr/ppermute | solution.py:19
  93.9 0.7 copy.65
  94.6 2.4 %collective-permute-start = (bf16[2,128,768]{1,2,0:T(8,128)(2,1)}, bf16[2,128,768]{1,2,0:T(8,128)(2,1)S(1)}, u32[]{:S(2)}, u32[]{:S(2)}) collective-permute-start(bf16[2,128,768]{1,2,0:T(8,128)(2,1)} %get-tuple-element.481), channel_id=1, source_target_pairs={{0,1},{1,2},{2,3},{3,4},{4,5},{5,6},{6,7},{7,8},{8,9},{9,10},{10,1... | collective-permute-start | bytes 1179656 | tf_op jit(solution)/shard_map/while/body/eval_jaxpr/ppermute | solution.py:19
  97.0 0.6 fusion.67
  99.5 2.5 %collective-permute-done = bf16[2,128,768]{1,2,0:T(8,128)(2,1)S(1)} collective-permute-done((bf16[2,128,768]{1,2,0:T(8,128)(2,1)}, bf16[2,128,768]{1,2,0:T(8,128)(2,1)S(1)}, u32[]{:S(2)}, u32[]{:S(2)}) %collective-permute-start) | collective-permute-done | bytes 393248 | tf_op jit(solution)/shard_map/while/body/eval_jaxpr/ppermute | solution.py:19
  102.8 0.7 copy.65
  103.6 2.4 %collective-permute-start = (bf16[2,128,768]{1,2,0:T(8,128)(2,1)}, bf16[2,128,768]{1,2,0:T(8,128)(2,1)S(1)}, u32[]{:S(2)}, u32[]{:S(2)}) collective-permute-start(bf16[2,128,768]{1,2,0:T(8,128)(2,1)} %get-tuple-element.481), channel_id=1, source_target_pairs={{0,1},{1,2},{2,3},{3,4},{4,5},{5,6},{6,7},{7,8},{8,9},{9,10},{10,1... | collective-permute-start | bytes 1179656 | tf_op jit(solution)/shard_map/while/body/eval_jaxpr/ppermute | solution.py:19
  106.0 0.6 fusion.67
  108.5 2.5 %collective-permute-done = bf16[2,128,768]{1,2,0:T(8,128)(2,1)S(1)} collective-permute-done((bf16[2,128,768]{1,2,0:T(8,128)(2,1)}, bf16[2,128,768]{1,2,0:T(8,128)(2,1)S(1)}, u32[]{:S(2)}, u32[]{:S(2)}) %collective-permute-start) | collective-permute-done | bytes 393248 | tf_op jit(solution)/shard_map/while/body/eval_jaxpr/ppermute | solution.py:19
  111.8 0.7 copy.65
  112.5 2.4 %collective-permute-start = (bf16[2,128,768]{1,2,0:T(8,128)(2,1)}, bf16[2,128,768]{1,2,0:T(8,128)(2,1)S(1)}, u32[]{:S(2)}, u32[]{:S(2)}) collective-permute-start(bf16[2,128,768]{1,2,0:T(8,128)(2,1)} %get-tuple-element.481), channel_id=1, source_target_pairs={{0,1},{1,2},{2,3},{3,4},{4,5},{5,6},{6,7},{7,8},{8,9},{9,10},{10,1... | collective-permute-start | bytes 1179656 | tf_op jit(solution)/shard_map/while/body/eval_jaxpr/ppermute | solution.py:19
  114.9 0.6 fusion.67
  117.4 2.5 %collective-permute-done = bf16[2,128,768]{1,2,0:T(8,128)(2,1)S(1)} collective-permute-done((bf16[2,128,768]{1,2,0:T(8,128)(2,1)}, bf16[2,128,768]{1,2,0:T(8,128)(2,1)S(1)}, u32[]{:S(2)}, u32[]{:S(2)}) %collective-permute-start) | collective-permute-done | bytes 393248 | tf_op jit(solution)/shard_map/while/body/eval_jaxpr/ppermute | solution.py:19
  120.7 0.7 copy.65
  122.2 1.4 gather_fusion.2
  123.6 1.0 broadcast_select_fusion.1
  124.6 18.5 %all-to-all-start.1 = ((bf16[16,16,1536]{2,1,0:T(8,128)(2,1)}), bf16[16,16,1536]{2,1,0:T(8,128)(2,1)S(1)}, u32[]{:S(2)}, u32[]{:S(2)}) async-start(bf16[16,16,1536]{2,1,0:T(8,128)(2,1)} %broadcast_select_fusion.1), calls=%async_computation.1 | async-start | bytes 1572864 | tf_op jit(solution)/shard_map/all_to_all | solution.py:156
  143.4 19.4 %all-to-all-done.1 = bf16[16,16,1536]{2,1,0:T(8,128)(2,1)S(1)} async-done(((bf16[16,16,1536]{2,1,0:T(8,128)(2,1)}), bf16[16,16,1536]{2,1,0:T(8,128)(2,1)S(1)}, u32[]{:S(2)}, u32[]{:S(2)}) %all-to-all-start.1) | async-done | bytes 786464 | tf_op jit(solution)/shard_map/all_to_all | solution.py:156
  162.8 0.9 gather_fusion.3
  163.7 0.9 broadcast_select_fusion.3
  (115 shorter events, 13.4 us)
Async XLA Ops:
  0.0 121.7 %copy-start = (bf16[768,1536]{1,0:T(8,128)(2,1)S(1)}, bf16[768,1536]{1,0:T(8,128)(2,1)}, u32[]{:S(2)}) copy-start(bf16[768,1536]{1,0:T(8,128)(2,1)} %param.11) | copy-start | bytes 7077892
  1.1 0.5 copy-start.10
  7.4 6.7 %copy-start.14 = (s32[2,16]{1,0:T(2,128)S(1)}, s32[2,16]{1,0:T(2,128)}, u32[]{:S(2)}) copy-start(s32[2,16]{1,0:T(2,128)} %param.9) | copy-start | bytes 388
  7.4 12.1 %copy-start.4 = (s32[16,16]{1,0:T(8,128)S(1)}, s32[16,16]{1,0:T(8,128)}, u32[]{:S(2)}) copy-start(s32[16,16]{1,0:T(8,128)} %param.8) | copy-start | bytes 3076
  7.4 34.3 %all-to-all-start = ((bf16[16,16,2304]{2,1,0:T(8,128)(2,1)}), bf16[16,16,2304]{2,1,0:T(8,128)(2,1)S(1)}, u32[]{:S(2)}, u32[]{:S(2)}) async-start(bf16[16,16,2304]{2,1,0:T(8,128)(2,1)} %broadcast_select_fusion), calls=%async_computation | async-start | bytes 2359296 | tf_op jit(solution)/shard_map/all_to_all | solution.py:80
  16.3 3.3 %copy-start.12 = (s32[1,16]{1,0:T(1,128)}, s32[1,16]{1,0:T(1,128)S(1)}, u32[]{:S(2)}) copy-start(s32[1,16]{1,0:T(1,128)S(1)} %get-tuple-element.469) | copy-start | bytes 196
  21.7 0.5 copy-start.8
  45.8 1.8 %copy-start.1 = (bf16[1,128,768]{2,1,0:T(8,128)(2,1)S(1)}, bf16[1,128,768]{2,1,0:T(8,128)(2,1)}, u32[]{:S(2)}) copy-start(bf16[1,128,768]{2,1,0:T(8,128)(2,1)} %get-tuple-element.362) | copy-start | bytes 589828
  45.8 3.2 %copy-start.5 = (s32[1,7]{1,0:T(1,128)S(1)}, s32[1,7]{1,0:T(1,128)}, u32[]{:S(2)}) copy-start(s32[1,7]{1,0:T(1,128)} %param.10) | copy-start | bytes 88
  45.8 5.1 %copy-start.9 = (s32[16]{0:T(128)S(1)}, s32[16]{0:T(128)}, u32[]{:S(2)}) copy-start(s32[16]{0:T(128)} %copy-done.8) | copy-start | bytes 196
  47.4 4.2 %copy-start.2 = (bf16[128,6,2,1,32]{0,4,3,2,1:T(8,128)(2,1)S(1)}, bf16[128,6,2,1,32]{0,4,3,2,1:T(8,128)(2,1)}, u32[]{:S(2)}) copy-start(bf16[128,6,2,1,32]{0,4,3,2,1:T(8,128)(2,1)} %get-tuple-element.364) | copy-start | bytes 294916
  47.4 4.2 %copy-start.3 = (bf16[128,6,2,1,32]{0,4,3,2,1:T(8,128)(2,1)S(1)}, bf16[128,6,2,1,32]{0,4,3,2,1:T(8,128)(2,1)}, u32[]{:S(2)}) copy-start(bf16[128,6,2,1,32]{0,4,3,2,1:T(8,128)(2,1)} %get-tuple-element.365) | copy-start | bytes 294916
  48.4 11.3 %collective-permute-start.1 = (bf16[2,128,768]{2,1,0:T(8,128)(2,1)}, bf16[2,128,768]{2,1,0:T(8,128)(2,1)S(1)}, u32[]{:S(2)}, u32[]{:S(2)}) collective-permute-start(bf16[2,128,768]{2,1,0:T(8,128)(2,1)} %pad_maximum_fusion), channel_id=1, source_target_pairs={{0,13},{1,14},{2,15},{3,0},{4,1},{5,2},{6,3},{7,4},{8,5},{9,6},{10... | collective-permute-start | bytes 1179656 | tf_op jit(solution)/shard_map/ppermute | solution.py:19
  65.8 2.1 %copy-start.6 = (s32[1,7]{1,0:T(1,128)S(1)}, s32[1,7]{1,0:T(1,128)}, u32[]{:S(2)}) copy-start(s32[1,7]{1,0:T(1,128)} %param.10) | copy-start | bytes 88
  65.8 2.1 %copy-start.13 = (s32[1,16]{1,0:T(1,128)S(1)}, s32[1,16]{1,0:T(1,128)}, u32[]{:S(2)}) copy-start(s32[1,16]{1,0:T(1,128)} %copy-done.12) | copy-start | bytes 196
  68.0 7.2 %collective-permute-start = (bf16[2,128,768]{1,2,0:T(8,128)(2,1)}, bf16[2,128,768]{1,2,0:T(8,128)(2,1)S(1)}, u32[]{:S(2)}, u32[]{:S(2)}) collective-permute-start(bf16[2,128,768]{1,2,0:T(8,128)(2,1)} %get-tuple-element.481), channel_id=1, source_target_pairs={{0,1},{1,2},{2,3},{3,4},{4,5},{5,6},{6,7},{7,8},{8,9},{9,10},{10,1... | collective-permute-start | bytes 1179656 | tf_op jit(solution)/shard_map/while/body/eval_jaxpr/ppermute | solution.py:19
  76.7 7.4 %collective-permute-start = (bf16[2,128,768]{1,2,0:T(8,128)(2,1)}, bf16[2,128,768]{1,2,0:T(8,128)(2,1)S(1)}, u32[]{:S(2)}, u32[]{:S(2)}) collective-permute-start(bf16[2,128,768]{1,2,0:T(8,128)(2,1)} %get-tuple-element.481), channel_id=1, source_target_pairs={{0,1},{1,2},{2,3},{3,4},{4,5},{5,6},{6,7},{7,8},{8,9},{9,10},{10,1... | collective-permute-start | bytes 1179656 | tf_op jit(solution)/shard_map/while/body/eval_jaxpr/ppermute | solution.py:19
  85.7 7.4 %collective-permute-start = (bf16[2,128,768]{1,2,0:T(8,128)(2,1)}, bf16[2,128,768]{1,2,0:T(8,128)(2,1)S(1)}, u32[]{:S(2)}, u32[]{:S(2)}) collective-permute-start(bf16[2,128,768]{1,2,0:T(8,128)(2,1)} %get-tuple-element.481), channel_id=1, source_target_pairs={{0,1},{1,2},{2,3},{3,4},{4,5},{5,6},{6,7},{7,8},{8,9},{9,10},{10,1... | collective-permute-start | bytes 1179656 | tf_op jit(solution)/shard_map/while/body/eval_jaxpr/ppermute | solution.py:19
  94.6 7.4 %collective-permute-start = (bf16[2,128,768]{1,2,0:T(8,128)(2,1)}, bf16[2,128,768]{1,2,0:T(8,128)(2,1)S(1)}, u32[]{:S(2)}, u32[]{:S(2)}) collective-permute-start(bf16[2,128,768]{1,2,0:T(8,128)(2,1)} %get-tuple-element.481), channel_id=1, source_target_pairs={{0,1},{1,2},{2,3},{3,4},{4,5},{5,6},{6,7},{7,8},{8,9},{9,10},{10,1... | collective-permute-start | bytes 1179656 | tf_op jit(solution)/shard_map/while/body/eval_jaxpr/ppermute | solution.py:19
  103.6 7.4 %collective-permute-start = (bf16[2,128,768]{1,2,0:T(8,128)(2,1)}, bf16[2,128,768]{1,2,0:T(8,128)(2,1)S(1)}, u32[]{:S(2)}, u32[]{:S(2)}) collective-permute-start(bf16[2,128,768]{1,2,0:T(8,128)(2,1)} %get-tuple-element.481), channel_id=1, source_target_pairs={{0,1},{1,2},{2,3},{3,4},{4,5},{5,6},{6,7},{7,8},{8,9},{9,10},{10,1... | collective-permute-start | bytes 1179656 | tf_op jit(solution)/shard_map/while/body/eval_jaxpr/ppermute | solution.py:19
  112.5 7.4 %collective-permute-start = (bf16[2,128,768]{1,2,0:T(8,128)(2,1)}, bf16[2,128,768]{1,2,0:T(8,128)(2,1)S(1)}, u32[]{:S(2)}, u32[]{:S(2)}) collective-permute-start(bf16[2,128,768]{1,2,0:T(8,128)(2,1)} %get-tuple-element.481), channel_id=1, source_target_pairs={{0,1},{1,2},{2,3},{3,4},{4,5},{5,6},{6,7},{7,8},{8,9},{9,10},{10,1... | collective-permute-start | bytes 1179656 | tf_op jit(solution)/shard_map/while/body/eval_jaxpr/ppermute | solution.py:19
  122.2 1.4 copy-start.7
  124.6 18.5 %copy-start.11 = (s32[16]{0:T(128)S(1)}, s32[16]{0:T(128)}, u32[]{:S(2)}) copy-start(s32[16]{0:T(128)} %copy-done.10) | copy-start | bytes 196
  124.6 38.1 %all-to-all-start.1 = ((bf16[16,16,1536]{2,1,0:T(8,128)(2,1)}), bf16[16,16,1536]{2,1,0:T(8,128)(2,1)S(1)}, u32[]{:S(2)}, u32[]{:S(2)}) async-start(bf16[16,16,1536]{2,1,0:T(8,128)(2,1)} %broadcast_select_fusion.1), calls=%async_computation.1 | async-start | bytes 1572864 | tf_op jit(solution)/shard_map/all_to_all | solution.py:156
where the time goes:
time: 165 us
  waiting for transfers between devices  57.5 us (35%)
  starting transfers between devices  39.3 us (24%)
  other arithmetic  27.2 us (16%)
  local copies, waits for them, and re-layouts  21.9 us (13%)
  loops' own time  7.9 us (5%)
  matrix products  7.06 us (4%)
  between operations  3.53 us (2%)
    ppermute x7, waiting for transfers between devices, from_behind(): return lax.ppermute(value, axis, pairs)  23 us
    all_to_all x1, waiting for transfers between devices, shards(): lax.all_to_all(returning, 'inner', split_axis=0, concat_axis=0, tiled=True)  19.4 us
    all_to_all x1, starting transfers between devices, shards(): lax.all_to_all(returning, 'inner', split_axis=0, concat_axis=0, tiled=True)  18.5 us
    all_to_all x1, waiting for transfers between devices, shards(): lax.all_to_all(parcels, 'inner', split_axis=0, concat_axis=0, tiled=True)  15.2 us
    ppermute x7, starting transfers between devices, from_behind(): return lax.ppermute(value, axis, pairs)  14.1 us
    another operation x1, loops' own time, shards(): lax.fori_loop(0, 2 * reach_count, one_way, (farthest, softmax_state))[1]  7.9 us
    all_to_all x1, starting transfers between devices, shards(): lax.all_to_all(parcels, 'inner', split_axis=0, concat_axis=0, tiled=True)  6.74 us
    reduce_sum x8, other arithmetic, block_places(): image_id = jnp.sum(inside, axis=1) - 1  5.9 us
  transfers between devices with their start and end apart: 9, of which 9 were waited for; matrix products, arithmetic and copies ran while one was open for 12% of the time, Pallas kernels for 0%

commit v1 on v0

--- a/solution.py
+++ b/solution.py
@@ -11,6 +11,22 @@
 SPAN = 4
 MAXT = 4
 WIN = 7
+
+
+def swapped_with_each(shard, axis, split, join):
+    ways, here = (lax.axis_size(axis), lax.axis_index(axis))
+    width = shard.shape[split] // ways
+    dims = list(shard.shape)
+    dims[split] = width
+    height = dims[join]
+    dims[join] = height * ways
+    full = jnp.zeros(dims, shard.dtype)
+    for mask in range(ways):
+        part = lax.dynamic_slice_in_dim(shard, (here ^ mask) * width, width, axis=split)
+        if mask:
+            part = lax.ppermute(part, axis, [(d, d ^ mask) for d in range(ways)])
+        full = lax.dynamic_update_slice_in_dim(full, part, (here ^ mask) * height, axis=join)
+    return full
 
 
 def from_behind(value, axis, steps):
@@ -153,7 +169,7 @@
     out_width = projected.shape[1]
     back_slots = jnp.minimum(taken_start[:, None] + slot_ids[None, :], tok_rows - 1).reshape(-1)
     returning = jnp.take(projected, back_slots, axis=0).reshape(devices, slot_count, out_width)
-    returned = lax.all_to_all(returning, "inner", split_axis=0, concat_axis=0, tiled=True)
+    returned = swapped_with_each(returning, "inner", 0, 0)
     target = jnp.sum((sent_end[None, :] <= row_ids[:, None]).astype(jnp.int32), axis=1)
     is_target = target[:, None] == peer_ids[None, :]
     offset_back = row_ids - jnp.sum(jnp.where(is_target, sent_start[None, :], 0), axis=1)

time: 165 us -> 170 us (1.030); the launches traced: 165 us -> 168 us
  starting transfers between devices: 39.3 us -> 52 us
  waiting for transfers between devices: 57.5 us -> 50.4 us
    ppermute x0 -> x15, starting transfers between devices: none -> 31.1 us  [swapped_with_each(): part = lax.ppermute(part, axis, [(d, d ^ mask) for d in range(ways)])]
    all_to_all x1 -> x0, waiting for transfers between devices: 19.4 us -> none  [shards(): lax.all_to_all(returning, 'inner', split_axis=0, concat_axis=0, tiled=True)]
    all_to_all x1 -> x0, starting transfers between devices: 18.5 us -> none  [shards(): lax.all_to_all(returning, 'inner', split_axis=0, concat_axis=0, tiled=True)]
    ppermute x0 -> x15, waiting for transfers between devices: none -> 8.75 us  [swapped_with_each(): part = lax.ppermute(part, axis, [(d, d ^ mask) for d in range(ways)])]
    all_to_all x1, waiting for transfers between devices: 15.2 us -> 19 us  [shards(): lax.all_to_all(parcels, 'inner', split_axis=0, concat_axis=0, tiled=True)]
  transfers between devices with their start and end apart: 9 -> 23, of which waited for: 9 -> 11; matrix products, arithmetic and copies ran while one was open for 12% -> 10% of each run, Pallas kernels for 0% -> 0%
where the time goes in v1:
time: 170 us; the launch traced here: 168 us
  starting transfers between devices  52 us (31%)
  waiting for transfers between devices  50.4 us (30%)
  other arithmetic  26.6 us (16%)
  local copies, waits for them, and re-layouts  20.7 us (12%)
  loops' own time  7.96 us (5%)
  matrix products  6.38 us (4%)
  between operations  3.57 us (2%)
    ppermute x15, starting transfers between devices, swapped_with_each(): part = lax.ppermute(part, axis, [(d, d ^ mask) for d in range(ways)])  31.1 us
    ppermute x7, waiting for transfers between devices, from_behind(): return lax.ppermute(value, axis, pairs)  22.7 us
    all_to_all x1, waiting for transfers between devices, shards(): lax.all_to_all(parcels, 'inner', split_axis=0, concat_axis=0, tiled=True)  19 us
    ppermute x7, starting transfers between devices, from_behind(): return lax.ppermute(value, axis, pairs)  14.1 us
    ppermute x15, waiting for transfers between devices, swapped_with_each(): part = lax.ppermute(part, axis, [(d, d ^ mask) for d in range(ways)])  8.75 us
    another operation x1, loops' own time, shards(): lax.fori_loop(0, 2 * reach_count, one_way, (farthest, softmax_state))[1]  7.96 us
    all_to_all x1, starting transfers between devices, shards(): lax.all_to_all(parcels, 'inner', split_axis=0, concat_axis=0, tiled=True)  6.74 us
    reduce_sum x8, other arithmetic, block_places(): image_id = jnp.sum(inside, axis=1) - 1  6.01 us
  transfers between devices with their start and end apart: 23, of which 11 were waited for; matrix products, arithmetic and copies ran while one was open for 10% of the time, Pallas kernels for 0%

profile of v1, /device:TPU:11, one launch (start us, length us, event | category | flops | bytes accessed | tf_op | source)
XLA Modules:
  0.0 167.6 jit_solution(5525317768762960952)
XLA Ops:
  0.0 0.8 fusion.36
  0.8 0.8 constant_dynamic-slice_fusion.16
  1.9 0.7 bitcast_subtract_fusion.3
  2.7 1.4 subtract_reduce_fusion
  4.1 0.7 compare_and_fusion
  5.6 3.7 %gather_fusion = bf16[256,2304]{1,0:T(8,128)(2,1)S(1)} fusion(bf16[128,2304]{1,0:T(8,128)(2,1)} %param.7, s32[1024]{0:T(1024)S(1)} %pad_clamp_fusion.3), kind=kCustom, calls=%fused_computation | custom fusion | bytes 2360320 | tf_op jit(solution)/shard_map/jit(_take)/gather | solution.py:95
  9.3 1.2 broadcast_select_fusion
  10.5 6.7 %all-to-all-start = ((bf16[16,16,2304]{2,1,0:T(8,128)(2,1)}), bf16[16,16,2304]{2,1,0:T(8,128)(2,1)S(1)}, u32[]{:S(2)}, u32[]{:S(2)}) async-start(bf16[16,16,2304]{2,1,0:T(8,128)(2,1)} %broadcast_select_fusion), calls=%async_computation | async-start | bytes 2359296 | tf_op jit(solution)/shard_map/all_to_all | solution.py:96
  17.2 0.8 reduce-window_2_clone.1
  18.0 1.3 fusion.28
  20.0 0.7 fusion.29
  21.3 0.7 fusion.27
  23.6 0.7 fusion.32
  24.5 0.8 fusion.21
  25.8 19.0 %all-to-all-done = bf16[16,16,2304]{2,1,0:T(8,128)(2,1)S(1)} async-done(((bf16[16,16,2304]{2,1,0:T(8,128)(2,1)}), bf16[16,16,2304]{2,1,0:T(8,128)(2,1)S(1)}, u32[]{:S(2)}, u32[]{:S(2)}) %all-to-all-start) | async-done | bytes 1179680 | tf_op jit(solution)/shard_map/all_to_all | solution.py:96
  44.8 1.8 %gather_fusion.1 = bf16[128,2304]{1,0:T(8,128)(2,1)} fusion(bf16[256,2304]{1,0:T(8,128)(2,1)S(1)} %bitcast.110, s32[1024]{0:T(1024)S(1)} %pad_clamp_fusion.2), kind=kCustom, calls=%fused_computation.1 | custom fusion | bytes 1180160 | tf_op jit(solution)/shard_map/jit(_take)/gather | solution.py:101
  46.5 1.2 broadcast_select_fusion.2
  47.7 0.7 slice_convert_fusion
  48.8 1.6 subtract_convert_fusion
  50.6 0.8 pad_maximum_fusion
  54.7 8.1 %collective-permute-done.1 = bf16[2,128,768]{2,1,0:T(8,128)(2,1)S(1)} collective-permute-done((bf16[2,128,768]{2,1,0:T(8,128)(2,1)}, bf16[2,128,768]{2,1,0:T(8,128)(2,1)S(1)}, u32[]{:S(2)}, u32[]{:S(2)}) %collective-permute-start.1) | collective-permute-done | bytes 393248 | tf_op jit(solution)/shard_map/ppermute | solution.py:35
  62.7 0.7 fusion.41
  63.4 0.8 copy.38
  64.2 1.2 fusion.42
  65.5 1.1 copy.42
  66.6 1.0 fusion.11
  67.6 1.2 copy.45
  68.8 0.9 copy.44
  69.7 53.5 %while.24 = (s32[]{:T(128)}, bf16[2,128,768]{1,2,0:T(8,128)(2,1)}, f32[128,6]{0,1:T(8,128)S(1)}, f32[128,6]{0,1:T(8,128)S(1)}, f32[128,6,128]{2,0,1:T(8,128)S(1)...) while((s32[]{:T(128)}, bf16[2,128,768]{1,2,0:T(8,128)(2,1)}, ...), condition=%wide.region_17.18_spmd, body=%wide.region_13.17_spmd.sunk | while | flops 51414596 | bytes 5751247 | solution.py:163
  69.7 2.2 %collective-permute-start = (bf16[2,128,768]{1,2,0:T(8,128)(2,1)}, bf16[2,128,768]{1,2,0:T(8,128)(2,1)S(1)}, u32[]{:S(2)}, u32[]{:S(2)}) collective-permute-start(bf16[2,128,768]{1,2,0:T(8,128)(2,1)} %get-tuple-element.501), channel_id=1, source_target_pairs={{0,1},{1,2},{2,3},{3,4},{4,5},{5,6},{6,7},{7,8},{8,9},{9,10},{10,1... | collective-permute-start | bytes 1179656 | tf_op jit(solution)/shard_map/while/body/eval_jaxpr/ppermute | solution.py:35
  74.5 2.4 %collective-permute-done = bf16[2,128,768]{1,2,0:T(8,128)(2,1)S(1)} collective-permute-done((bf16[2,128,768]{1,2,0:T(8,128)(2,1)}, bf16[2,128,768]{1,2,0:T(8,128)(2,1)S(1)}, u32[]{:S(2)}, u32[]{:S(2)}) %collective-permute-start) | collective-permute-done | bytes 393248 | tf_op jit(solution)/shard_map/while/body/eval_jaxpr/ppermute | solution.py:35
  77.7 0.7 copy.65
  78.5 2.4 %collective-permute-start = (bf16[2,128,768]{1,2,0:T(8,128)(2,1)}, bf16[2,128,768]{1,2,0:T(8,128)(2,1)S(1)}, u32[]{:S(2)}, u32[]{:S(2)}) collective-permute-start(bf16[2,128,768]{1,2,0:T(8,128)(2,1)} %get-tuple-element.501), channel_id=1, source_target_pairs={{0,1},{1,2},{2,3},{3,4},{4,5},{5,6},{6,7},{7,8},{8,9},{9,10},{10,1... | collective-permute-start | bytes 1179656 | tf_op jit(solution)/shard_map/while/body/eval_jaxpr/ppermute | solution.py:35
  83.4 2.4 %collective-permute-done = bf16[2,128,768]{1,2,0:T(8,128)(2,1)S(1)} collective-permute-done((bf16[2,128,768]{1,2,0:T(8,128)(2,1)}, bf16[2,128,768]{1,2,0:T(8,128)(2,1)S(1)}, u32[]{:S(2)}, u32[]{:S(2)}) %collective-permute-start) | collective-permute-done | bytes 393248 | tf_op jit(solution)/shard_map/while/body/eval_jaxpr/ppermute | solution.py:35
  86.7 0.7 copy.65
  87.4 2.4 %collective-permute-start = (bf16[2,128,768]{1,2,0:T(8,128)(2,1)}, bf16[2,128,768]{1,2,0:T(8,128)(2,1)S(1)}, u32[]{:S(2)}, u32[]{:S(2)}) collective-permute-start(bf16[2,128,768]{1,2,0:T(8,128)(2,1)} %get-tuple-element.501), channel_id=1, source_target_pairs={{0,1},{1,2},{2,3},{3,4},{4,5},{5,6},{6,7},{7,8},{8,9},{9,10},{10,1... | collective-permute-start | bytes 1179656 | tf_op jit(solution)/shard_map/while/body/eval_jaxpr/ppermute | solution.py:35
  92.4 2.4 %collective-permute-done = bf16[2,128,768]{1,2,0:T(8,128)(2,1)S(1)} collective-permute-done((bf16[2,128,768]{1,2,0:T(8,128)(2,1)}, bf16[2,128,768]{1,2,0:T(8,128)(2,1)S(1)}, u32[]{:S(2)}, u32[]{:S(2)}) %collective-permute-start) | collective-permute-done | bytes 393248 | tf_op jit(solution)/shard_map/while/body/eval_jaxpr/ppermute | solution.py:35
  95.6 0.7 copy.65
  96.4 2.4 %collective-permute-start = (bf16[2,128,768]{1,2,0:T(8,128)(2,1)}, bf16[2,128,768]{1,2,0:T(8,128)(2,1)S(1)}, u32[]{:S(2)}, u32[]{:S(2)}) collective-permute-start(bf16[2,128,768]{1,2,0:T(8,128)(2,1)} %get-tuple-element.501), channel_id=1, source_target_pairs={{0,1},{1,2},{2,3},{3,4},{4,5},{5,6},{6,7},{7,8},{8,9},{9,10},{10,1... | collective-permute-start | bytes 1179656 | tf_op jit(solution)/shard_map/while/body/eval_jaxpr/ppermute | solution.py:35
  101.3 2.4 %collective-permute-done = bf16[2,128,768]{1,2,0:T(8,128)(2,1)S(1)} collective-permute-done((bf16[2,128,768]{1,2,0:T(8,128)(2,1)}, bf16[2,128,768]{1,2,0:T(8,128)(2,1)S(1)}, u32[]{:S(2)}, u32[]{:S(2)}) %collective-permute-start) | collective-permute-done | bytes 393248 | tf_op jit(solution)/shard_map/while/body/eval_jaxpr/ppermute | solution.py:35
  104.6 0.7 copy.65
  105.3 2.4 %collective-permute-start = (bf16[2,128,768]{1,2,0:T(8,128)(2,1)}, bf16[2,128,768]{1,2,0:T(8,128)(2,1)S(1)}, u32[]{:S(2)}, u32[]{:S(2)}) collective-permute-start(bf16[2,128,768]{1,2,0:T(8,128)(2,1)} %get-tuple-element.501), channel_id=1, source_target_pairs={{0,1},{1,2},{2,3},{3,4},{4,5},{5,6},{6,7},{7,8},{8,9},{9,10},{10,1... | collective-permute-start | bytes 1179656 | tf_op jit(solution)/shard_map/while/body/eval_jaxpr/ppermute | solution.py:35
  110.3 2.4 %collective-permute-done = bf16[2,128,768]{1,2,0:T(8,128)(2,1)S(1)} collective-permute-done((bf16[2,128,768]{1,2,0:T(8,128)(2,1)}, bf16[2,128,768]{1,2,0:T(8,128)(2,1)S(1)}, u32[]{:S(2)}, u32[]{:S(2)}) %collective-permute-start) | collective-permute-done | bytes 393248 | tf_op jit(solution)/shard_map/while/body/eval_jaxpr/ppermute | solution.py:35
  113.5 0.7 copy.65
  114.3 2.4 %collective-permute-start = (bf16[2,128,768]{1,2,0:T(8,128)(2,1)}, bf16[2,128,768]{1,2,0:T(8,128)(2,1)S(1)}, u32[]{:S(2)}, u32[]{:S(2)}) collective-permute-start(bf16[2,128,768]{1,2,0:T(8,128)(2,1)} %get-tuple-element.501), channel_id=1, source_target_pairs={{0,1},{1,2},{2,3},{3,4},{4,5},{5,6},{6,7},{7,8},{8,9},{9,10},{10,1... | collective-permute-start | bytes 1179656 | tf_op jit(solution)/shard_map/while/body/eval_jaxpr/ppermute | solution.py:35
  119.2 2.4 %collective-permute-done = bf16[2,128,768]{1,2,0:T(8,128)(2,1)S(1)} collective-permute-done((bf16[2,128,768]{1,2,0:T(8,128)(2,1)}, bf16[2,128,768]{1,2,0:T(8,128)(2,1)S(1)}, u32[]{:S(2)}, u32[]{:S(2)}) %collective-permute-start) | collective-permute-done | bytes 393248 | tf_op jit(solution)/shard_map/while/body/eval_jaxpr/ppermute | solution.py:35
  122.5 0.7 copy.65
  124.0 1.4 gather_fusion.2
  125.7 3.8 %collective-permute-start.2 = (bf16[1,16,1536]{2,1,0:T(8,128)(2,1)S(1)}, bf16[1,16,1536]{2,1,0:T(8,128)(2,1)S(1)}, u32[]{:S(2)}, u32[]{:S(2)}) collective-permute-start(bf16[1,16,1536]{2,1,0:T(8,128)(2,1)S(1)} %get-tuple-element.375), channel_id=1, source_target_pairs={{0,1},{1,0},{2,3},{3,2},{4,5},{5,4},{6,7},{7,6},{8,9},{9,8},{10,11... | collective-permute-start | bytes 147464 | tf_op jit(solution)/shard_map/ppermute | solution.py:27
  129.6 1.9 %collective-permute-start.4 = (bf16[1,16,1536]{2,1,0:T(8,128)(2,1)S(1)}, bf16[1,16,1536]{2,1,0:T(8,128)(2,1)S(1)}, u32[]{:S(2)}, u32[]{:S(2)}) collective-permute-start(bf16[1,16,1536]{2,1,0:T(8,128)(2,1)S(1)} %get-tuple-element.373), channel_id=1, source_target_pairs={{0,3},{1,2},{2,1},{3,0},{4,7},{5,6},{6,5},{7,4},{8,11},{9,10},{10,... | collective-permute-start | bytes 147464 | tf_op jit(solution)/shard_map/ppermute | solution.py:27
  131.5 11.3 %collective-permute-start.5 = (bf16[1,16,1536]{2,1,0:T(8,128)(2,1)S(1)}, bf16[1,16,1536]{2,1,0:T(8,128)(2,1)S(1)}, u32[]{:S(2)}, u32[]{:S(2)}) collective-permute-start(bf16[1,16,1536]{2,1,0:T(8,128)(2,1)S(1)} %get-tuple-element.372), channel_id=1, source_target_pairs={{0,4},{1,5},{2,6},{3,7},{4,0},{5,1},{6,2},{7,3},{8,12},{9,13},{10,... | collective-permute-start | bytes 147464 | tf_op jit(solution)/shard_map/ppermute | solution.py:27
  142.8 1.5 collective-permute-start.7
  144.3 1.6 collective-permute-start.8
  146.0 2.4 %collective-permute-start.10 = (bf16[1,16,1536]{2,1,0:T(8,128)(2,1)S(1)}, bf16[1,16,1536]{2,1,0:T(8,128)(2,1)S(1)}, u32[]{:S(2)}, u32[]{:S(2)}) collective-permute-start(bf16[1,16,1536]{2,1,0:T(8,128)(2,1)S(1)} %get-tuple-element.367), channel_id=1, source_target_pairs={{0,9},{1,8},{2,11},{3,10},{4,13},{5,12},{6,15},{7,14},{8,1},{9,0},... | collective-permute-start | bytes 147464 | tf_op jit(solution)/shard_map/ppermute | solution.py:27
  148.3 0.7 collective-permute-start.11
  149.0 3.3 %collective-permute-start.12 = (bf16[1,16,1536]{2,1,0:T(8,128)(2,1)S(1)}, bf16[1,16,1536]{2,1,0:T(8,128)(2,1)S(1)}, u32[]{:S(2)}, u32[]{:S(2)}) collective-permute-start(bf16[1,16,1536]{2,1,0:T(8,128)(2,1)S(1)} %get-tuple-element.365), channel_id=1, source_target_pairs={{0,11},{1,10},{2,9},{3,8},{4,15},{5,14},{6,13},{7,12},{8,3},{9,2},... | collective-permute-start | bytes 147464 | tf_op jit(solution)/shard_map/ppermute | solution.py:27
  152.7 1.2 collective-permute-start.14
  153.9 0.7 collective-permute-start.15
  154.7 2.4 %collective-permute-start.16 = (bf16[1,16,1536]{2,1,0:T(8,128)(2,1)S(1)}, bf16[1,16,1536]{2,1,0:T(8,128)(2,1)S(1)}, u32[]{:S(2)}, u32[]{:S(2)}) collective-permute-start(bf16[1,16,1536]{2,1,0:T(8,128)(2,1)S(1)} %get-tuple-element.361), channel_id=1, source_target_pairs={{0,15},{1,14},{2,13},{3,12},{4,11},{5,10},{6,9},{7,8},{8,7},{9,6},... | collective-permute-start | bytes 147464 | tf_op jit(solution)/shard_map/ppermute | solution.py:27
  157.1 5.0 %collective-permute-done.13 = bf16[1,16,1536]{2,1,0:T(8,128)(2,1)S(1)} collective-permute-done((bf16[1,16,1536]{2,1,0:T(8,128)(2,1)S(1)}, bf16[1,16,1536]{2,1,0:T(8,128)(2,1)S(1)}, u32[]{:S(2)}, u32[]{:S(2)}) %collective-permute-start.13) | collective-permute-done | bytes 49184 | tf_op jit(solution)/shard_map/ppermute | solution.py:27
  162.1 2.2 %collective-permute-done.14 = bf16[1,16,1536]{2,1,0:T(8,128)(2,1)S(1)} collective-permute-done((bf16[1,16,1536]{2,1,0:T(8,128)(2,1)S(1)}, bf16[1,16,1536]{2,1,0:T(8,128)(2,1)S(1)}, u32[]{:S(2)}, u32[]{:S(2)}) %collective-permute-start.14) | collective-permute-done | bytes 49184 | tf_op jit(solution)/shard_map/ppermute | solution.py:27
  164.3 1.5 collective-permute-done.16
  165.8 0.9 gather_fusion.3
  166.8 0.9 broadcast_select_fusion.3
  (156 shorter events, 19.4 us)
Async XLA Ops:
  0.0 123.4 %copy-start = (bf16[768,1536]{1,0:T(8,128)(2,1)S(1)}, bf16[768,1536]{1,0:T(8,128)(2,1)}, u32[]{:S(2)}) copy-start(bf16[768,1536]{1,0:T(8,128)(2,1)} %param.11) | copy-start | bytes 7077892
  10.5 6.7 %copy-start.9 = (s32[2,16]{1,0:T(2,128)S(1)}, s32[2,16]{1,0:T(2,128)}, u32[]{:S(2)}) copy-start(s32[2,16]{1,0:T(2,128)} %param.9) | copy-start | bytes 388
  10.5 34.3 %all-to-all-start = ((bf16[16,16,2304]{2,1,0:T(8,128)(2,1)}), bf16[16,16,2304]{2,1,0:T(8,128)(2,1)S(1)}, u32[]{:S(2)}, u32[]{:S(2)}) async-start(bf16[16,16,2304]{2,1,0:T(8,128)(2,1)} %broadcast_select_fusion), calls=%async_computation | async-start | bytes 2359296 | tf_op jit(solution)/shard_map/all_to_all | solution.py:96
  19.3 4.2 %copy-start.7 = (s32[1,16]{1,0:T(1,128)}, s32[1,16]{1,0:T(1,128)S(1)}, u32[]{:S(2)}) copy-start(s32[1,16]{1,0:T(1,128)S(1)} %get-tuple-element.489) | copy-start | bytes 196
  23.6 1.6 copy-start.12
  48.8 1.8 %copy-start.1 = (bf16[1,128,768]{2,1,0:T(8,128)(2,1)S(1)}, bf16[1,128,768]{2,1,0:T(8,128)(2,1)}, u32[]{:S(2)}) copy-start(bf16[1,128,768]{2,1,0:T(8,128)(2,1)} %get-tuple-element.378) | copy-start | bytes 589828
  48.8 2.6 %copy-start.6 = (s32[256,1]{0,1:T(1,128)S(1)}, s32[256,1]{0,1:T(1,128)}, u32[]{:S(2)}) copy-start(s32[256,1]{0,1:T(1,128)} %get-tuple-element.398) | copy-start | bytes 3076
  48.8 3.8 %copy-start.4 = (s32[1,7]{1,0:T(1,128)S(1)}, s32[1,7]{1,0:T(1,128)}, u32[]{:S(2)}) copy-start(s32[1,7]{1,0:T(1,128)} %param.10) | copy-start | bytes 88
  50.4 3.4 %copy-start.13 = (s32[128]{0:T(128)S(1)}, s32[128]{0:T(128)}, u32[]{:S(2)}) copy-start(s32[128]{0:T(128)} %copy-done.12) | copy-start | bytes 1540
  50.4 4.0 %copy-start.2 = (bf16[128,6,2,1,32]{0,4,3,2,1:T(8,128)(2,1)S(1)}, bf16[128,6,2,1,32]{0,4,3,2,1:T(8,128)(2,1)}, u32[]{:S(2)}) copy-start(bf16[128,6,2,1,32]{0,4,3,2,1:T(8,128)(2,1)} %get-tuple-element.380) | copy-start | bytes 294916
  50.4 4.0 %copy-start.3 = (bf16[128,6,2,1,32]{0,4,3,2,1:T(8,128)(2,1)S(1)}, bf16[128,6,2,1,32]{0,4,3,2,1:T(8,128)(2,1)}, u32[]{:S(2)}) copy-start(bf16[128,6,2,1,32]{0,4,3,2,1:T(8,128)(2,1)} %get-tuple-element.381) | copy-start | bytes 294916
  51.4 11.3 %collective-permute-start.1 = (bf16[2,128,768]{2,1,0:T(8,128)(2,1)}, bf16[2,128,768]{2,1,0:T(8,128)(2,1)S(1)}, u32[]{:S(2)}, u32[]{:S(2)}) collective-permute-start(bf16[2,128,768]{2,1,0:T(8,128)(2,1)} %pad_maximum_fusion), channel_id=1, source_target_pairs={{0,13},{1,14},{2,15},{3,0},{4,1},{5,2},{6,3},{7,4},{8,5},{9,6},{10... | collective-permute-start | bytes 1179656 | tf_op jit(solution)/shard_map/ppermute | solution.py:35
  67.6 2.1 %copy-start.8 = (s32[1,16]{1,0:T(1,128)S(1)}, s32[1,16]{1,0:T(1,128)}, u32[]{:S(2)}) copy-start(s32[1,16]{1,0:T(1,128)} %copy-done.7) | copy-start | bytes 196
  69.7 7.2 %collective-permute-start = (bf16[2,128,768]{1,2,0:T(8,128)(2,1)}, bf16[2,128,768]{1,2,0:T(8,128)(2,1)S(1)}, u32[]{:S(2)}, u32[]{:S(2)}) collective-permute-start(bf16[2,128,768]{1,2,0:T(8,128)(2,1)} %get-tuple-element.501), channel_id=1, source_target_pairs={{0,1},{1,2},{2,3},{3,4},{4,5},{5,6},{6,7},{7,8},{8,9},{9,10},{10,1... | collective-permute-start | bytes 1179656 | tf_op jit(solution)/shard_map/while/body/eval_jaxpr/ppermute | solution.py:35
  78.5 7.4 %collective-permute-start = (bf16[2,128,768]{1,2,0:T(8,128)(2,1)}, bf16[2,128,768]{1,2,0:T(8,128)(2,1)S(1)}, u32[]{:S(2)}, u32[]{:S(2)}) collective-permute-start(bf16[2,128,768]{1,2,0:T(8,128)(2,1)} %get-tuple-element.501), channel_id=1, source_target_pairs={{0,1},{1,2},{2,3},{3,4},{4,5},{5,6},{6,7},{7,8},{8,9},{9,10},{10,1... | collective-permute-start | bytes 1179656 | tf_op jit(solution)/shard_map/while/body/eval_jaxpr/ppermute | solution.py:35
  87.4 7.4 %collective-permute-start = (bf16[2,128,768]{1,2,0:T(8,128)(2,1)}, bf16[2,128,768]{1,2,0:T(8,128)(2,1)S(1)}, u32[]{:S(2)}, u32[]{:S(2)}) collective-permute-start(bf16[2,128,768]{1,2,0:T(8,128)(2,1)} %get-tuple-element.501), channel_id=1, source_target_pairs={{0,1},{1,2},{2,3},{3,4},{4,5},{5,6},{6,7},{7,8},{8,9},{9,10},{10,1... | collective-permute-start | bytes 1179656 | tf_op jit(solution)/shard_map/while/body/eval_jaxpr/ppermute | solution.py:35
  96.4 7.4 %collective-permute-start = (bf16[2,128,768]{1,2,0:T(8,128)(2,1)}, bf16[2,128,768]{1,2,0:T(8,128)(2,1)S(1)}, u32[]{:S(2)}, u32[]{:S(2)}) collective-permute-start(bf16[2,128,768]{1,2,0:T(8,128)(2,1)} %get-tuple-element.501), channel_id=1, source_target_pairs={{0,1},{1,2},{2,3},{3,4},{4,5},{5,6},{6,7},{7,8},{8,9},{9,10},{10,1... | collective-permute-start | bytes 1179656 | tf_op jit(solution)/shard_map/while/body/eval_jaxpr/ppermute | solution.py:35
  105.3 7.4 %collective-permute-start = (bf16[2,128,768]{1,2,0:T(8,128)(2,1)}, bf16[2,128,768]{1,2,0:T(8,128)(2,1)S(1)}, u32[]{:S(2)}, u32[]{:S(2)}) collective-permute-start(bf16[2,128,768]{1,2,0:T(8,128)(2,1)} %get-tuple-element.501), channel_id=1, source_target_pairs={{0,1},{1,2},{2,3},{3,4},{4,5},{5,6},{6,7},{7,8},{8,9},{9,10},{10,1... | collective-permute-start | bytes 1179656 | tf_op jit(solution)/shard_map/while/body/eval_jaxpr/ppermute | solution.py:35
  114.3 7.4 %collective-permute-start = (bf16[2,128,768]{1,2,0:T(8,128)(2,1)}, bf16[2,128,768]{1,2,0:T(8,128)(2,1)S(1)}, u32[]{:S(2)}, u32[]{:S(2)}) collective-permute-start(bf16[2,128,768]{1,2,0:T(8,128)(2,1)} %get-tuple-element.501), channel_id=1, source_target_pairs={{0,1},{1,2},{2,3},{3,4},{4,5},{5,6},{6,7},{7,8},{8,9},{9,10},{10,1... | collective-permute-start | bytes 1179656 | tf_op jit(solution)/shard_map/while/body/eval_jaxpr/ppermute | solution.py:35
  123.9 1.4 copy-start.5
  125.5 4.1 %copy-start.10 = (s32[128]{0:T(128)S(1)}, s32[128]{0:T(128)}, u32[]{:S(2)}) copy-start(s32[128]{0:T(128)} %fusion.31) | copy-start | bytes 1540
  125.7 17.1 %collective-permute-start.2 = (bf16[1,16,1536]{2,1,0:T(8,128)(2,1)S(1)}, bf16[1,16,1536]{2,1,0:T(8,128)(2,1)S(1)}, u32[]{:S(2)}, u32[]{:S(2)}) collective-permute-start(bf16[1,16,1536]{2,1,0:T(8,128)(2,1)S(1)} %get-tuple-element.375), channel_id=1, source_target_pairs={{0,1},{1,0},{2,3},{3,2},{4,5},{5,4},{6,7},{7,6},{8,9},{9,8},{10,11... | collective-permute-start | bytes 147464 | tf_op jit(solution)/shard_map/ppermute | solution.py:27
  129.6 14.7 %collective-permute-start.3 = (bf16[1,16,1536]{2,1,0:T(8,128)(2,1)S(1)}, bf16[1,16,1536]{2,1,0:T(8,128)(2,1)S(1)}, u32[]{:S(2)}, u32[]{:S(2)}) collective-permute-start(bf16[1,16,1536]{2,1,0:T(8,128)(2,1)S(1)} %get-tuple-element.374), channel_id=1, source_target_pairs={{0,2},{1,3},{2,0},{3,1},{4,6},{5,7},{6,4},{7,5},{8,10},{9,11},{10,... | collective-permute-start | bytes 147464 | tf_op jit(solution)/shard_map/ppermute | solution.py:27
  129.6 16.2 %collective-permute-start.4 = (bf16[1,16,1536]{2,1,0:T(8,128)(2,1)S(1)}, bf16[1,16,1536]{2,1,0:T(8,128)(2,1)S(1)}, u32[]{:S(2)}, u32[]{:S(2)}) collective-permute-start(bf16[1,16,1536]{2,1,0:T(8,128)(2,1)S(1)} %get-tuple-element.373), channel_id=1, source_target_pairs={{0,3},{1,2},{2,1},{3,0},{4,7},{5,6},{6,5},{7,4},{8,11},{9,10},{10,... | collective-permute-start | bytes 147464 | tf_op jit(solution)/shard_map/ppermute | solution.py:27
  131.5 14.4 %collective-permute-start.5 = (bf16[1,16,1536]{2,1,0:T(8,128)(2,1)S(1)}, bf16[1,16,1536]{2,1,0:T(8,128)(2,1)S(1)}, u32[]{:S(2)}, u32[]{:S(2)}) collective-permute-start(bf16[1,16,1536]{2,1,0:T(8,128)(2,1)S(1)} %get-tuple-element.372), channel_id=1, source_target_pairs={{0,4},{1,5},{2,6},{3,7},{4,0},{5,1},{6,2},{7,3},{8,12},{9,13},{10,... | collective-permute-start | bytes 147464 | tf_op jit(solution)/shard_map/ppermute | solution.py:27
  142.8 5.5 %collective-permute-start.6 = (bf16[1,16,1536]{2,1,0:T(8,128)(2,1)S(1)}, bf16[1,16,1536]{2,1,0:T(8,128)(2,1)S(1)}, u32[]{:S(2)}, u32[]{:S(2)}) collective-permute-start(bf16[1,16,1536]{2,1,0:T(8,128)(2,1)S(1)} %get-tuple-element.371), channel_id=1, source_target_pairs={{0,5},{1,4},{2,7},{3,6},{4,1},{5,0},{6,3},{7,2},{8,13},{9,12},{10,... | collective-permute-start | bytes 147464 | tf_op jit(solution)/shard_map/ppermute | solution.py:27
  142.8 6.2 %collective-permute-start.7 = (bf16[1,16,1536]{2,1,0:T(8,128)(2,1)S(1)}, bf16[1,16,1536]{2,1,0:T(8,128)(2,1)S(1)}, u32[]{:S(2)}, u32[]{:S(2)}) collective-permute-start(bf16[1,16,1536]{2,1,0:T(8,128)(2,1)S(1)} %get-tuple-element.370), channel_id=1, source_target_pairs={{0,6},{1,7},{2,4},{3,5},{4,2},{5,3},{6,0},{7,1},{8,14},{9,15},{10,... | collective-permute-start | bytes 147464 | tf_op jit(solution)/shard_map/ppermute | solution.py:27
  144.3 8.1 %collective-permute-start.8 = (bf16[1,16,1536]{2,1,0:T(8,128)(2,1)S(1)}, bf16[1,16,1536]{2,1,0:T(8,128)(2,1)S(1)}, u32[]{:S(2)}, u32[]{:S(2)}) collective-permute-start(bf16[1,16,1536]{2,1,0:T(8,128)(2,1)S(1)} %get-tuple-element.369), channel_id=1, source_target_pairs={{0,7},{1,6},{2,5},{3,4},{4,3},{5,2},{6,1},{7,0},{8,15},{9,14},{10,... | collective-permute-start | bytes 147464 | tf_op jit(solution)/shard_map/ppermute | solution.py:27
  145.8 6.9 %collective-permute-start.9 = (bf16[1,16,1536]{2,1,0:T(8,128)(2,1)S(1)}, bf16[1,16,1536]{2,1,0:T(8,128)(2,1)S(1)}, u32[]{:S(2)}, u32[]{:S(2)}) collective-permute-start(bf16[1,16,1536]{2,1,0:T(8,128)(2,1)S(1)} %get-tuple-element.368), channel_id=1, source_target_pairs={{0,8},{1,9},{2,10},{3,11},{4,12},{5,13},{6,14},{7,15},{8,0},{9,1},... | collective-permute-start | bytes 147464 | tf_op jit(solution)/shard_map/ppermute | solution.py:27
  146.0 8.0 %collective-permute-start.10 = (bf16[1,16,1536]{2,1,0:T(8,128)(2,1)S(1)}, bf16[1,16,1536]{2,1,0:T(8,128)(2,1)S(1)}, u32[]{:S(2)}, u32[]{:S(2)}) collective-permute-start(bf16[1,16,1536]{2,1,0:T(8,128)(2,1)S(1)} %get-tuple-element.367), channel_id=1, source_target_pairs={{0,9},{1,8},{2,11},{3,10},{4,13},{5,12},{6,15},{7,14},{8,1},{9,0},... | collective-permute-start | bytes 147464 | tf_op jit(solution)/shard_map/ppermute | solution.py:27
  148.3 6.3 %collective-permute-start.11 = (bf16[1,16,1536]{2,1,0:T(8,128)(2,1)S(1)}, bf16[1,16,1536]{2,1,0:T(8,128)(2,1)S(1)}, u32[]{:S(2)}, u32[]{:S(2)}) collective-permute-start(bf16[1,16,1536]{2,1,0:T(8,128)(2,1)S(1)} %get-tuple-element.366), channel_id=1, source_target_pairs={{0,10},{1,11},{2,8},{3,9},{4,14},{5,15},{6,12},{7,13},{8,2},{9,3},... | collective-permute-start | bytes 147464 | tf_op jit(solution)/shard_map/ppermute | solution.py:27
  149.0 8.0 %collective-permute-start.12 = (bf16[1,16,1536]{2,1,0:T(8,128)(2,1)S(1)}, bf16[1,16,1536]{2,1,0:T(8,128)(2,1)S(1)}, u32[]{:S(2)}, u32[]{:S(2)}) collective-permute-start(bf16[1,16,1536]{2,1,0:T(8,128)(2,1)S(1)} %get-tuple-element.365), channel_id=1, source_target_pairs={{0,11},{1,10},{2,9},{3,8},{4,15},{5,14},{6,13},{7,12},{8,3},{9,2},... | collective-permute-start | bytes 147464 | tf_op jit(solution)/shard_map/ppermute | solution.py:27
  152.4 9.8 %collective-permute-start.13 = (bf16[1,16,1536]{2,1,0:T(8,128)(2,1)S(1)}, bf16[1,16,1536]{2,1,0:T(8,128)(2,1)S(1)}, u32[]{:S(2)}, u32[]{:S(2)}) collective-permute-start(bf16[1,16,1536]{2,1,0:T(8,128)(2,1)S(1)} %get-tuple-element.364), channel_id=1, source_target_pairs={{0,12},{1,13},{2,14},{3,15},{4,8},{5,9},{6,10},{7,11},{8,4},{9,5},... | collective-permute-start | bytes 147464 | tf_op jit(solution)/shard_map/ppermute | solution.py:27
  152.7 11.6 %collective-permute-start.14 = (bf16[1,16,1536]{2,1,0:T(8,128)(2,1)S(1)}, bf16[1,16,1536]{2,1,0:T(8,128)(2,1)S(1)}, u32[]{:S(2)}, u32[]{:S(2)}) collective-permute-start(bf16[1,16,1536]{2,1,0:T(8,128)(2,1)S(1)} %get-tuple-element.363), channel_id=1, source_target_pairs={{0,13},{1,12},{2,15},{3,14},{4,9},{5,8},{6,11},{7,10},{8,5},{9,4},... | collective-permute-start | bytes 147464 | tf_op jit(solution)/shard_map/ppermute | solution.py:27
  153.9 10.4 %collective-permute-start.15 = (bf16[1,16,1536]{2,1,0:T(8,128)(2,1)S(1)}, bf16[1,16,1536]{2,1,0:T(8,128)(2,1)S(1)}, u32[]{:S(2)}, u32[]{:S(2)}) collective-permute-start(bf16[1,16,1536]{2,1,0:T(8,128)(2,1)S(1)} %get-tuple-element.362), channel_id=1, source_target_pairs={{0,14},{1,15},{2,12},{3,13},{4,10},{5,11},{6,8},{7,9},{8,6},{9,7},... | collective-permute-start | bytes 147464 | tf_op jit(solution)/shard_map/ppermute | solution.py:27
  154.7 11.2 %collective-permute-start.16 = (bf16[1,16,1536]{2,1,0:T(8,128)(2,1)S(1)}, bf16[1,16,1536]{2,1,0:T(8,128)(2,1)S(1)}, u32[]{:S(2)}, u32[]{:S(2)}) collective-permute-start(bf16[1,16,1536]{2,1,0:T(8,128)(2,1)S(1)} %get-tuple-element.361), channel_id=1, source_target_pairs={{0,15},{1,14},{2,13},{3,12},{4,11},{5,10},{6,9},{7,8},{8,7},{9,6},... | collective-permute-start | bytes 147464 | tf_op jit(solution)/shard_map/ppermute | solution.py:27
  165.8 0.9 copy-start.11
